TPU v7x, 512 devices: a whole 4x8x8 slice. The times are simulated.
512 devices in a mesh: row: 16 (over z, core), col: 32 (over y, x).
Axes of the slice: x: 4, y: 8, z: 8, core: 2. Of those that a mesh axis runs over, the one named last changes fastest.
Arguments:
- train_embed: bfloat16 [8192, 256], P(('row', 'col')), may hold values from -16 to 16
- valid_embed: bfloat16 [65536, 256], P(('row', 'col')), may hold values from -16 to 16
- train_labels: int32 [8192], P(('row', 'col')), may hold values from 0 to 99
- valid_labels: int32 [65536], P(('row', 'col')), may hold values from 0 to 99
- pair_level: int32 [100, 100], replicated, may hold values from 0 to 3
- level_cost: float32 [4], replicated, may hold values from 0.05 to 1
Outputs:
- calibrated: float32 [8192], P('row')
All inputs are finite; a program needn't handle non-finite values.
Results may differ from a plain program's by a relative error of at most 0.0003.
Values may be sent and summed in bfloat16 or wider, within the bound.
No kernel may reach another device: no remote copies, remote signals or barrier semaphores. Data moves between devices by JAX's collectives and lax.ppermute only.
A program may use at most 64 MiB of HBM per device.

v0:
```python
import math
import jax
import jax.numpy as jnp
from jax import lax
from jax.sharding import PartitionSpec as P

ITERS = 4
entropy_scale = 0.05


def inner_products(left_rows, right_rows):
    return lax.dot_general(
        left_rows, right_rows, (((1,), (1,)), ((), ())), preferred_element_type=jnp.float32
    )


def squared_norms(embeddings):
    widened = embeddings.astype(jnp.float32)
    return jnp.sum(widened * widened, axis=1)


def class_costs(pair_level, level_cost):
    num_levels = level_cost.shape[0]
    selected = (
        pair_level[:, :, None] == jnp.arange(num_levels, dtype=jnp.int32)[None, None, :]
    ).astype(jnp.float32)
    return jnp.sum(selected * level_cost[None, None, :], axis=2)


def label_costs(row_labels, class_ids, labels_y):
    col_hot = (class_ids[:, None] == labels_y[None, :]).astype(jnp.float32)
    return jnp.dot(
        row_labels, col_hot, precision=lax.Precision.HIGHEST, preferred_element_type=jnp.float32
    )


def shards(train_embed, valid_embed, train_labels, valid_labels, pair_level, level_cost):
    rows_x, labels_x = (
        lax.all_gather(train_embed, "col", axis=0, tiled=True),
        lax.all_gather(train_labels, "col", axis=0, tiled=True),
    )
    width_d = rows_x.shape[1]
    classes = pair_level.shape[0]
    class_table = class_costs(pair_level, level_cost)
    class_ids = jnp.arange(classes, dtype=jnp.int32)
    train_hot = (labels_x[:, None] == class_ids[None, :]).astype(jnp.float32)
    row_labels = jnp.dot(
        train_hot, class_table, precision=lax.Precision.HIGHEST, preferred_element_type=jnp.float32
    )
    train_sq = squared_norms(rows_x)
    cols_y, labels_y = (
        lax.all_gather(valid_embed, "row", axis=0, tiled=True),
        lax.all_gather(valid_labels, "row", axis=0, tiled=True),
    )
    valid_sq = squared_norms(cols_y)
    label_full = label_costs(row_labels, class_ids, labels_y)

    def cost_block(offset, block_cols):
        block_y = lax.dynamic_slice_in_dim(cols_y, offset, block_cols, 0)
        block_sq = lax.dynamic_slice_in_dim(valid_sq, offset, block_cols, 0)
        label_slice = lax.dynamic_slice_in_dim(label_full, offset, block_cols, 1)
        return (
            train_sq[:, None] + block_sq[None, :] - 2.0 * inner_products(rows_x, block_y)
        ) / width_d + label_slice

    row_count = rows_x.shape[0]
    col_count = labels_y.shape[0]
    block_cols = min(512, col_count)
    block_count = col_count // block_cols
    block_ids = jnp.arange(block_count, dtype=jnp.int32)

    def scores(block_index, row_pot, col_pot):
        offset = block_index * block_cols
        cost_tile = cost_block(offset, block_cols)
        block_pot = lax.dynamic_slice_in_dim(col_pot, offset, block_cols, 0)
        return (
            (block_pot[None, :] - cost_tile) / entropy_scale,
            (row_pot[:, None] - cost_tile) / entropy_scale,
        )

    row_pot = jnp.zeros((row_count,), jnp.float32)
    col_pot = jnp.zeros((col_count,), jnp.float32)
    full_rows = row_count * lax.axis_size("row")
    full_cols = col_count * lax.axis_size("col")
    for iteration in range(ITERS):

        def local_peaks(running, block_index, row_pot=row_pot, col_pot=col_pot):
            row_side, col_side = scores(block_index, row_pot, col_pot)
            return (jnp.maximum(running, jnp.max(row_side, axis=1)), jnp.max(col_side, axis=0))

        row_local, col_local = lax.scan(
            local_peaks, jnp.full((row_count,), -jnp.inf, jnp.float32), block_ids
        )
        row_high = lax.pmax(row_local, "col")
        col_high = lax.pmax(col_local.reshape(col_count), "row")

        def local_totals(
            running,
            block_index,
            row_pot=row_pot,
            col_pot=col_pot,
            row_high=row_high,
            col_high=col_high,
        ):
            row_side, col_side = scores(block_index, row_pot, col_pot)
            block_high = lax.dynamic_slice_in_dim(col_high, block_index * block_cols, block_cols, 0)
            return (
                running + jnp.sum(jnp.exp(row_side - row_high[:, None]), axis=1),
                jnp.sum(jnp.exp(col_side - block_high[None, :]), axis=0),
            )

        row_part, col_part = lax.scan(local_totals, jnp.zeros((row_count,), jnp.float32), block_ids)
        row_sum = lax.psum(row_part, "col")
        col_sum = lax.psum(col_part.reshape(col_count), "row")
        row_new = entropy_scale * math.log(full_cols) - entropy_scale * (
            row_high + jnp.log(row_sum)
        )
        col_new = entropy_scale * math.log(full_rows) - entropy_scale * (
            col_high + jnp.log(col_sum)
        )
        row_pot = 0.5 * (row_pot + row_new)
        col_pot = 0.5 * (col_pot + col_new)
    potential_sum = lax.psum(jnp.sum(row_pot), "row")
    return (row_pot * full_rows - potential_sum) / (full_rows - 1)


def solution(mesh):
    placed = (
        P(("row", "col"), None),
        P(("row", "col"), None),
        P(("row", "col")),
        P(("row", "col")),
        P(),
        P(),
    )
    return jax.shard_map(shards, mesh=mesh, in_specs=placed, out_specs=P("row"), check_vma=False)
```

profile of v0, /device:TPU:1, one launch (start us, length us, event | category | flops | bytes accessed | tf_op | source)
XLA Modules:
  0.0 894.9 jit_solution(5116224132933514768)
XLA Ops:
  10.3 17.5 %all-reduce = s32[512]{0:T(512)S(1)} all-reduce(s32[512]{0:T(512)S(1)} %dynamic-update-slice), channel_id=1, replica_groups=mesh['row'=16,'col'=32] {'col'}, use_global_device_ids=true, to_apply=%add | all-reduce | flops 512 | bytes 4096
  27.7 28.0 %all-gather = s32[16,1,128]{2,1,0:T(1,128)S(1)} all-gather(s32[1,1,128]{2,1,0:T(1,128)} %bitcast.194), channel_id=1, replica_groups=mesh['row'=16,'col'=32] {'row'}, dimensions={0}, use_global_device_ids=true | all-gather | bytes 8704 | tf_op jit(solution)/shard_map/all_gather | solution.py:53
  55.7 34.7 %all_gather.12 = bf16[512,256]{1,0:T(8,128)(2,1)S(1)} all-gather(bf16[16,256]{1,0:T(8,128)(2,1)} %param.22), channel_id=1, replica_groups=mesh['row'=16,'col'=32] {'col'}, dimensions={0}, use_global_device_ids=true | all-gather | bytes 270336 | tf_op jit(solution)/shard_map/all_gather | solution.py:39
  92.0 3.8 fusion.60
  97.4 13.7 %while.100 = (s32[]{:T(128)}, f32[512]{0:T(512)S(1)}, f32[4,512]{1,0:T(4,128)S(1)}, f32[512]{0:T(512)S(1)}, s32[4]{0:T(128)S(1)}, /*index=5*/f32[2048]{0:T(1024)...) while((s32[]{:T(128)}, f32[512]{0:T(512)S(1)}, ...), condition=%wide.region_6.7_spmd.clone, body=%wide.region_3.6_spmd.clone.sunk | while | flops 136577024 | bytes 1596617 | solution.py:91
  111.1 36.0 %pmax.50 = f32[2048]{0:T(1024)S(1)} all-reduce(f32[2048]{0:T(1024)S(1)} %bitcast.188), channel_id=1, replica_groups=mesh['row'=16,'col'=32] {'row'}, use_global_device_ids=true, to_apply=%region_8.9 | all-reduce | flops 2048 | bytes 16384 | tf_op jit(solution)/shard_map/pmax | solution.py:95
  147.1 58.1 %pmax.49 = f32[512]{0:T(512)S(1)} all-reduce(f32[512]{0:T(512)S(1)} %get-tuple-element.462), channel_id=1, replica_groups=mesh['row'=16,'col'=32] {'col'}, use_global_device_ids=true, to_apply=%region_7.8 | all-reduce | flops 512 | bytes 4096 | tf_op jit(solution)/shard_map/pmax | solution.py:94
  205.2 14.1 %while.101 = (s32[]{:T(128)}, f32[512]{0:T(512)S(1)}, f32[4,512]{1,0:T(4,128)S(1)}, f32[512]{0:T(512)S(1)}, s32[4]{0:T(128)S(1)}, /*index=5*/f32[2048]{0:T(1024)...) while((s32[]{:T(128)}, f32[512]{0:T(512)S(1)}, ...), condition=%wide.region_12.13_spmd.clone, body=%wide.region_9.12_spmd.clone.sunk | while | flops 137101312 | bytes 1604829 | solution.py:112
  206.6 2.1 exponential_reduce_fusion.9
  210.1 2.1 exponential_reduce_fusion.9
  213.6 2.1 exponential_reduce_fusion.9
  217.1 2.1 exponential_reduce_fusion.9
  219.3 56.1 %psum.56 = f32[512]{0:T(512)S(1)} all-reduce(f32[512]{0:T(512)S(1)} %get-tuple-element.464), channel_id=1, replica_groups=mesh['row'=16,'col'=32] {'col'}, use_global_device_ids=true, to_apply=%region_13.14 | all-reduce | flops 512 | bytes 4096 | tf_op jit(solution)/shard_map/psum | solution.py:113
  275.5 51.8 %psum.57 = f32[2048]{0:T(1024)S(1)} all-reduce(f32[2048]{0:T(1024)S(1)} %bitcast.189), channel_id=1, replica_groups=mesh['row'=16,'col'=32] {'row'}, use_global_device_ids=true, to_apply=%region_14.15 | all-reduce | flops 2048 | bytes 16384 | tf_op jit(solution)/shard_map/psum | solution.py:114
  327.3 13.7 %while.102 = (s32[]{:T(128)}, f32[512]{0:T(512)S(1)}, f32[4,512]{1,0:T(4,128)S(1)}, s32[4]{0:T(128)S(1)}, f32[2048]{0:T(1024)S(1)}, /*index=5*/f32[512]{0:T(512)...) while((s32[]{:T(128)}, f32[512]{0:T(512)S(1)}, ...), condition=%wide.region_18.19_spmd.clone, body=%wide.region_15.18_spmd.clone.sunk | while | flops 137101312 | bytes 1604829 | solution.py:91
  328.7 2.0 multiply_reduce_fusion.9
  332.1 2.0 multiply_reduce_fusion.9
  335.5 2.0 multiply_reduce_fusion.9
  339.0 2.0 multiply_reduce_fusion.9
  341.0 24.0 %pmax.52 = f32[2048]{0:T(1024)S(1)} all-reduce(f32[2048]{0:T(1024)S(1)} %bitcast.190), channel_id=1, replica_groups=mesh['row'=16,'col'=32] {'row'}, use_global_device_ids=true, to_apply=%region_20.21 | all-reduce | flops 2048 | bytes 16384 | tf_op jit(solution)/shard_map/pmax | solution.py:95
  365.1 57.4 %pmax.51 = f32[512]{0:T(512)S(1)} all-reduce(f32[512]{0:T(512)S(1)} %get-tuple-element.466), channel_id=1, replica_groups=mesh['row'=16,'col'=32] {'col'}, use_global_device_ids=true, to_apply=%region_19.20 | all-reduce | flops 512 | bytes 4096 | tf_op jit(solution)/shard_map/pmax | solution.py:94
  422.5 14.9 %while.103 = (s32[]{:T(128)}, f32[512]{0:T(512)S(1)}, f32[4,512]{1,0:T(4,128)S(1)}, s32[4]{0:T(128)S(1)}, f32[2048]{0:T(1024)S(1)}, /*index=5*/f32[512]{0:T(512)...) while((s32[]{:T(128)}, f32[512]{0:T(512)S(1)}, ...), condition=%wide.region_24.25_spmd.clone, body=%wide.region_21.24_spmd.clone.sunk | while | flops 137625600 | bytes 1613041 | solution.py:112
  424.0 2.2 exponential_reduce_fusion.10
  427.7 2.2 exponential_reduce_fusion.10
  431.4 2.2 exponential_reduce_fusion.10
  435.2 2.2 exponential_reduce_fusion.10
  437.4 56.1 %psum.58 = f32[512]{0:T(512)S(1)} all-reduce(f32[512]{0:T(512)S(1)} %get-tuple-element.468), channel_id=1, replica_groups=mesh['row'=16,'col'=32] {'col'}, use_global_device_ids=true, to_apply=%region_25.26 | all-reduce | flops 512 | bytes 4096 | tf_op jit(solution)/shard_map/psum | solution.py:113
  493.6 51.8 %psum.59 = f32[2048]{0:T(1024)S(1)} all-reduce(f32[2048]{0:T(1024)S(1)} %bitcast.191), channel_id=1, replica_groups=mesh['row'=16,'col'=32] {'row'}, use_global_device_ids=true, to_apply=%region_26.27 | all-reduce | flops 2048 | bytes 16384 | tf_op jit(solution)/shard_map/psum | solution.py:114
  545.4 13.5 %while.104 = (s32[]{:T(128)}, f32[512]{0:T(512)S(1)}, f32[4,512]{1,0:T(4,128)S(1)}, s32[4]{0:T(128)S(1)}, f32[2048]{0:T(1024)S(1)}, /*index=5*/f32[512]{0:T(512)...) while((s32[]{:T(128)}, f32[512]{0:T(512)S(1)}, ...), condition=%wide.region_30.31_spmd.clone, body=%wide.region_27.30_spmd.clone.sunk | while | flops 137101312 | bytes 1604829 | solution.py:91
  546.7 2.0 multiply_reduce_fusion.10
  550.1 2.0 multiply_reduce_fusion.10
  553.4 2.0 multiply_reduce_fusion.10
  556.8 2.0 multiply_reduce_fusion.10
  558.8 24.1 %pmax.54 = f32[2048]{0:T(1024)S(1)} all-reduce(f32[2048]{0:T(1024)S(1)} %bitcast.192), channel_id=1, replica_groups=mesh['row'=16,'col'=32] {'row'}, use_global_device_ids=true, to_apply=%region_32.33 | all-reduce | flops 2048 | bytes 16384 | tf_op jit(solution)/shard_map/pmax | solution.py:95
  582.9 57.4 %pmax.53 = f32[512]{0:T(512)S(1)} all-reduce(f32[512]{0:T(512)S(1)} %get-tuple-element.470), channel_id=1, replica_groups=mesh['row'=16,'col'=32] {'col'}, use_global_device_ids=true, to_apply=%region_31.32 | all-reduce | flops 512 | bytes 4096 | tf_op jit(solution)/shard_map/pmax | solution.py:94
  640.3 15.5 %while.105 = (s32[]{:T(128)}, f32[512]{0:T(512)S(1)}, f32[4,512]{1,0:T(4,128)S(1)}, s32[4]{0:T(128)S(1)}, f32[2048]{0:T(1024)S(1)}, /*index=5*/f32[512]{0:T(512)...) while((s32[]{:T(128)}, f32[512]{0:T(512)S(1)}, ...), condition=%wide.region_36.37_spmd.clone, body=%wide.region_33.36_spmd.clone.sunk | while | flops 137625600 | bytes 1613041 | solution.py:112
  641.9 2.2 exponential_reduce_fusion.11
  645.8 2.2 exponential_reduce_fusion.11
  649.7 2.2 exponential_reduce_fusion.11
  653.5 2.2 exponential_reduce_fusion.11
  655.8 38.2 %psum.61 = f32[2048]{0:T(1024)S(1)} all-reduce(f32[2048]{0:T(1024)S(1)} %bitcast.193), channel_id=1, replica_groups=mesh['row'=16,'col'=32] {'row'}, use_global_device_ids=true, to_apply=%region_38.39 | all-reduce | flops 2048 | bytes 16384 | tf_op jit(solution)/shard_map/psum | solution.py:114
  694.1 13.1 %while.106 = (s32[]{:T(128)}, f32[512]{0:T(512)S(1)}, s32[4]{0:T(128)S(1)}, f32[2048]{0:T(1024)S(1)}, f32[512]{0:T(512)S(1)}, /*index=5*/f32[2048]{0:T(1024)S(1)...) while((s32[]{:T(128)}, f32[512]{0:T(512)S(1)}, ...), condition=%wide.region_41.42_spmd.clone, body=%wide.region_39.41_spmd.clone.sunk | while | flops 136315392 | bytes 1596617 | solution.py:91
  707.3 55.7 %pmax.55 = f32[512]{0:T(512)S(1)} all-reduce(f32[512]{0:T(512)S(1)} %get-tuple-element.474), channel_id=1, replica_groups=mesh['row'=16,'col'=32] {'col'}, use_global_device_ids=true, to_apply=%region_42.43 | all-reduce | flops 512 | bytes 4096 | tf_op jit(solution)/shard_map/pmax | solution.py:94
  763.0 13.4 %while.107 = (s32[]{:T(128)}, f32[512]{0:T(512)S(1)}, s32[4]{0:T(128)S(1)}, f32[2048]{0:T(1024)S(1)}, f32[512]{0:T(512)S(1)}, /*index=5*/f32[2048]{0:T(1024)S(1)...) while((s32[]{:T(128)}, f32[512]{0:T(512)S(1)}, ...), condition=%wide.region_45.46_spmd.clone, body=%wide.region_43.45_spmd.clone.sunk | while | flops 136577536 | bytes 1598673 | solution.py:112
  764.4 1.9 fusion.100
  774.4 1.9 fusion.100
  776.4 57.7 %all-reduce.1 = (f32[512]{0:T(512)S(1)}, f32[512]{0:T(512)S(1)}) all-reduce(f32[512]{0:T(512)S(1)} %get-tuple-element.475, f32[512]{0:T(512)S(1)} %get-tuple-element.472), channel_id=1, replica_groups=mesh['row'=16,'col'=32] {'col'}, use_global_device_ids=true, to_apply=%region_46.47 | all-reduce | flops 1024 | bytes 8192 | tf_op jit(solution)/shard_map/psum | solution.py:113
  834.7 52.1 %psum.63 = f32[]{:T(128)} all-reduce(f32[]{:T(128)} %get-tuple-element.1210), channel_id=1, replica_groups=mesh['row'=16,'col'=32] {'row'}, use_global_device_ids=true, to_apply=%region_48.49 | all-reduce | flops 1 | bytes 8 | tf_op jit(solution)/shard_map/psum | solution.py:123
  (211 shorter events, 53.3 us)
Async XLA Ops:
  6.5 89.3 %all-gather.3.cloned.1.call-start = ((), (), s32[]{:S(2)}) async-start(), calls=%async_computation | async-start | bytes 1114112 | tf_op jit(solution)/shard_map/all_gather | solution.py:52
Sparse Core Ops, SparseCore 0:
  9.5 48.0 all-gather.2
where the time goes:
time: 897 us; the launch traced here: 895 us
  blocking collectives  757 us (84%)
  matrix products  68.1 us (8%)
  local copies, waits for them, and re-layouts  28.5 us (3%)
  loops' own time  21.2 us (2%)
  between operations  14.4 us (2%)
    pmax x4, blocking collectives, shards(): row_high = lax.pmax(row_local, 'col')  229 us
    psum x3, blocking collectives, shards(): row_sum = lax.psum(row_part, 'col')  170 us
    psum x3, blocking collectives, shards(): col_sum = lax.psum(col_part.reshape(col_count), 'row')  142 us
    pmax x3, blocking collectives, shards(): col_high = lax.pmax(col_local.reshape(col_count), 'row')  84.1 us
    dot_general x32, matrix products, inner_products(): lax.dot_general(left_rows, right_rows, (((1,), (1,)), ((), ())), preferre...  64 us
    psum x1, blocking collectives, shards(): potential_sum = lax.psum(jnp.sum(row_pot), 'row')  52.1 us
    all_gather x1, blocking collectives, shards(): lax.all_gather(train_embed, 'col', axis=0, tiled=True)  34.7 us
    all_gather x1, blocking collectives, shards(): lax.all_gather(valid_labels, 'row', axis=0, tiled=True)  28 us
  transfers between devices with their start and end apart: 1, of which 0 were waited for; matrix products, arithmetic and copies ran while one was open for 1% of the time, Pallas kernels for 0%

commit v1 on v0

--- a/solution.py
+++ b/solution.py
@@ -6,6 +6,18 @@
 
 ITERS = 4
 entropy_scale = 0.05
+
+
+def begin_spans_on_mesh(page):
+    extra, state_now = (page, 0)
+    extent = jax.lax.axis_size("col")
+    while 1 << state_now < extent:
+        frame_out = jax.lax.ppermute(
+            extra, axis_name="col", perm=[(nth, nth ^ 1 << state_now) for nth in range(extent)]
+        )
+        extra = extra + frame_out
+        state_now = state_now + 1
+    return extra
 
 
 def inner_products(left_rows, right_rows):
@@ -110,7 +122,7 @@
             )
 
         row_part, col_part = lax.scan(local_totals, jnp.zeros((row_count,), jnp.float32), block_ids)
-        row_sum = lax.psum(row_part, "col")
+        row_sum = begin_spans_on_mesh(row_part)
         col_sum = lax.psum(col_part.reshape(col_count), "row")
         row_new = entropy_scale * math.log(full_cols) - entropy_scale * (
             row_high + jnp.log(row_sum)

time: 897 us -> 784 us (0.87)
  blocking collectives: 757 us -> 560 us
  starting transfers between devices: 0.01 us -> 56 us
  waiting for transfers between devices: 0.71 us -> 28.1 us
    psum x3 -> x0, blocking collectives: 170 us -> none  [shards(): row_sum = lax.psum(row_part, 'col')]
    ppermute x0 -> x20, starting transfers between devices: none -> 56 us  [begin_spans_on_mesh(): jax.lax.ppermute(extra, axis_name='col', perm=[(nth, nth ^ 1 << state_now...]
    ppermute x0 -> x20, waiting for transfers between devices: none -> 27.4 us  [begin_spans_on_mesh(): jax.lax.ppermute(extra, axis_name='col', perm=[(nth, nth ^ 1 << state_now...]
    psum x3, blocking collectives: 142 us -> 122 us  [shards(): col_sum = lax.psum(col_part.reshape(col_count), 'row')]
    psum x1, blocking collectives: 52.1 us -> 41.6 us  [shards(): potential_sum = lax.psum(jnp.sum(row_pot), 'row')]
  transfers between devices with their start and end apart: 1 -> 21, of which waited for: 0 -> 10; matrix products, arithmetic and copies ran while one was open for 1% -> 4% of each run, Pallas kernels for 0% -> 0%
where the time goes in v1:
time: 784 us; the launch traced here: 782 us
  blocking collectives  560 us (71%)
  matrix products  68.1 us (9%)
  starting transfers between devices  56 us (7%)
  local copies, waits for them, and re-layouts  28.6 us (4%)
  waiting for transfers between devices  28.1 us (4%)
  loops' own time  21.4 us (3%)
  between operations  14.7 us (2%)
    pmax x4, blocking collectives, shards(): row_high = lax.pmax(row_local, 'col')  230 us
    psum x3, blocking collectives, shards(): col_sum = lax.psum(col_part.reshape(col_count), 'row')  122 us
    pmax x3, blocking collectives, shards(): col_high = lax.pmax(col_local.reshape(col_count), 'row')  86.4 us
    dot_general x32, matrix products, inner_products(): lax.dot_general(left_rows, right_rows, (((1,), (1,)), ((), ())), preferre...  64 us
    ppermute x20, starting transfers between devices, begin_spans_on_mesh(): jax.lax.ppermute(extra, axis_name='col', perm=[(nth, nth ^ 1 << state_now...  56 us
    psum x1, blocking collectives, shards(): potential_sum = lax.psum(jnp.sum(row_pot), 'row')  41.6 us
    all_gather x1, blocking collectives, shards(): lax.all_gather(train_embed, 'col', axis=0, tiled=True)  34.7 us
    all_gather x1, blocking collectives, shards(): lax.all_gather(valid_labels, 'row', axis=0, tiled=True)  28 us
  transfers between devices with their start and end apart: 21, of which 10 were waited for; matrix products, arithmetic and copies ran while one was open for 4% of the time, Pallas kernels for 0%

profile of v1, /device:TPU:1, one launch (start us, length us, event | category | flops | bytes accessed | tf_op | source)
XLA Modules:
  0.0 782.3 jit_solution(4030312618932380438)
XLA Ops:
  10.2 17.5 %all-reduce = s32[512]{0:T(512)S(1)} all-reduce(s32[512]{0:T(512)S(1)} %dynamic-update-slice), channel_id=1, replica_groups=mesh['row'=16,'col'=32] {'col'}, use_global_device_ids=true, to_apply=%add | all-reduce | flops 512 | bytes 4096
  27.7 28.0 %all-gather = s32[16,1,128]{2,1,0:T(1,128)S(1)} all-gather(s32[1,1,128]{2,1,0:T(1,128)} %bitcast.194), channel_id=1, replica_groups=mesh['row'=16,'col'=32] {'row'}, dimensions={0}, use_global_device_ids=true | all-gather | bytes 8704 | tf_op jit(solution)/shard_map/all_gather | solution.py:65
  55.7 34.7 %all_gather.12 = bf16[512,256]{1,0:T(8,128)(2,1)S(1)} all-gather(bf16[16,256]{1,0:T(8,128)(2,1)} %param.22), channel_id=1, replica_groups=mesh['row'=16,'col'=32] {'col'}, dimensions={0}, use_global_device_ids=true | all-gather | bytes 270336 | tf_op jit(solution)/shard_map/all_gather | solution.py:51
  92.0 3.8 fusion.60
  97.4 13.4 %while.100 = (s32[]{:T(128)}, f32[512]{0:T(512)S(1)}, f32[4,512]{1,0:T(4,128)S(1)}, f32[512]{0:T(512)S(1)}, s32[4]{0:T(128)S(1)}, /*index=5*/f32[2048]{0:T(1024)...) while((s32[]{:T(128)}, f32[512]{0:T(512)S(1)}, ...), condition=%wide.region_6.7_spmd.clone, body=%wide.region_3.6_spmd.clone.sunk | while | flops 136577024 | bytes 1596617 | solution.py:103
  110.8 36.0 %pmax.50 = f32[2048]{0:T(1024)S(1)} all-reduce(f32[2048]{0:T(1024)S(1)} %bitcast.190), channel_id=1, replica_groups=mesh['row'=16,'col'=32] {'row'}, use_global_device_ids=true, to_apply=%region_8.9 | all-reduce | flops 2048 | bytes 16384 | tf_op jit(solution)/shard_map/pmax | solution.py:107
  146.8 58.1 %pmax.49 = f32[512]{0:T(512)S(1)} all-reduce(f32[512]{0:T(512)S(1)} %get-tuple-element.462), channel_id=1, replica_groups=mesh['row'=16,'col'=32] {'col'}, use_global_device_ids=true, to_apply=%region_7.8 | all-reduce | flops 512 | bytes 4096 | tf_op jit(solution)/shard_map/pmax | solution.py:106
  204.9 14.4 %while.101 = (s32[]{:T(128)}, f32[512]{0:T(512)S(1)}, f32[4,512]{1,0:T(4,128)S(1)}, f32[512]{0:T(512)S(1)}, s32[4]{0:T(128)S(1)}, /*index=5*/f32[2048]{0:T(1024)...) while((s32[]{:T(128)}, f32[512]{0:T(512)S(1)}, ...), condition=%wide.region_12.13_spmd.clone, body=%wide.region_9.12_spmd.clone.sunk | while | flops 137101312 | bytes 1604829 | solution.py:124
  206.3 2.1 exponential_reduce_fusion.9
  221.3 2.4 collective-permute-done
  225.6 3.9 collective-permute-done.1
  231.4 2.4 collective-permute-done.2
  235.7 41.7 %psum.28 = f32[2048]{0:T(1024)S(1)} all-reduce(f32[2048]{0:T(1024)S(1)} %bitcast.182), channel_id=1, replica_groups=mesh['row'=16,'col'=32] {'row'}, use_global_device_ids=true, to_apply=%region_13.14 | all-reduce | flops 2048 | bytes 16384 | tf_op jit(solution)/shard_map/psum | solution.py:126
  277.4 5.9 collective-permute-start.4
  283.3 2.3 collective-permute-done.4
  285.7 13.9 %while.102 = (s32[]{:T(128)}, f32[512]{0:T(512)S(1)}, f32[4,512]{1,0:T(4,128)S(1)}, s32[4]{0:T(128)S(1)}, f32[2048]{0:T(1024)S(1)}, /*index=5*/f32[512]{0:T(512)...) while((s32[]{:T(128)}, f32[512]{0:T(512)S(1)}, ...), condition=%wide.region_17.18_spmd.clone, body=%wide.region_14.17_spmd.clone.sunk | while | flops 137101312 | bytes 1604829 | solution.py:103
  299.6 25.2 %pmax.52 = f32[2048]{0:T(1024)S(1)} all-reduce(f32[2048]{0:T(1024)S(1)} %bitcast.191), channel_id=1, replica_groups=mesh['row'=16,'col'=32] {'row'}, use_global_device_ids=true, to_apply=%region_19.20 | all-reduce | flops 2048 | bytes 16384 | tf_op jit(solution)/shard_map/pmax | solution.py:107
  324.8 57.4 %pmax.51 = f32[512]{0:T(512)S(1)} all-reduce(f32[512]{0:T(512)S(1)} %get-tuple-element.466), channel_id=1, replica_groups=mesh['row'=16,'col'=32] {'col'}, use_global_device_ids=true, to_apply=%region_18.19 | all-reduce | flops 512 | bytes 4096 | tf_op jit(solution)/shard_map/pmax | solution.py:106
  382.2 15.0 %while.103 = (s32[]{:T(128)}, f32[512]{0:T(512)S(1)}, f32[4,512]{1,0:T(4,128)S(1)}, s32[4]{0:T(128)S(1)}, f32[2048]{0:T(1024)S(1)}, /*index=5*/f32[512]{0:T(512)...) while((s32[]{:T(128)}, f32[512]{0:T(512)S(1)}, ...), condition=%wide.region_23.24_spmd.clone, body=%wide.region_20.23_spmd.clone.sunk | while | flops 137625600 | bytes 1613041 | solution.py:124
  383.7 2.2 exponential_reduce_fusion.10
  387.4 2.2 exponential_reduce_fusion.10
  391.2 2.2 exponential_reduce_fusion.10
  394.9 2.2 exponential_reduce_fusion.10
  399.1 2.4 collective-permute-done.5
  403.4 3.9 collective-permute-done.6
  409.3 2.4 collective-permute-done.7
  413.6 41.7 %psum.29 = f32[2048]{0:T(1024)S(1)} all-reduce(f32[2048]{0:T(1024)S(1)} %bitcast.183), channel_id=1, replica_groups=mesh['row'=16,'col'=32] {'row'}, use_global_device_ids=true, to_apply=%region_24.25 | all-reduce | flops 2048 | bytes 16384 | tf_op jit(solution)/shard_map/psum | solution.py:126
  455.3 3.9 collective-permute-start.9
  459.3 4.3 collective-permute-done.9
  463.6 13.4 %while.104 = (s32[]{:T(128)}, f32[512]{0:T(512)S(1)}, f32[4,512]{1,0:T(4,128)S(1)}, s32[4]{0:T(128)S(1)}, f32[2048]{0:T(1024)S(1)}, /*index=5*/f32[512]{0:T(512)...) while((s32[]{:T(128)}, f32[512]{0:T(512)S(1)}, ...), condition=%wide.region_28.29_spmd.clone, body=%wide.region_25.28_spmd.clone.sunk | while | flops 137101312 | bytes 1604829 | solution.py:103
  477.0 25.2 %pmax.54 = f32[2048]{0:T(1024)S(1)} all-reduce(f32[2048]{0:T(1024)S(1)} %bitcast.192), channel_id=1, replica_groups=mesh['row'=16,'col'=32] {'row'}, use_global_device_ids=true, to_apply=%region_30.31 | all-reduce | flops 2048 | bytes 16384 | tf_op jit(solution)/shard_map/pmax | solution.py:107
  502.3 57.4 %pmax.53 = f32[512]{0:T(512)S(1)} all-reduce(f32[512]{0:T(512)S(1)} %get-tuple-element.470), channel_id=1, replica_groups=mesh['row'=16,'col'=32] {'col'}, use_global_device_ids=true, to_apply=%region_29.30 | all-reduce | flops 512 | bytes 4096 | tf_op jit(solution)/shard_map/pmax | solution.py:106
  559.7 15.5 %while.105 = (s32[]{:T(128)}, f32[512]{0:T(512)S(1)}, f32[4,512]{1,0:T(4,128)S(1)}, s32[4]{0:T(128)S(1)}, f32[2048]{0:T(1024)S(1)}, /*index=5*/f32[512]{0:T(512)...) while((s32[]{:T(128)}, f32[512]{0:T(512)S(1)}, ...), condition=%wide.region_34.35_spmd.clone, body=%wide.region_31.34_spmd.clone.sunk | while | flops 137625600 | bytes 1613041 | solution.py:124
  561.3 2.2 exponential_reduce_fusion.11
  565.2 2.2 exponential_reduce_fusion.11
  569.0 2.2 exponential_reduce_fusion.11
  572.9 2.2 exponential_reduce_fusion.11
  577.1 38.2 %psum.30 = f32[2048]{0:T(1024)S(1)} all-reduce(f32[2048]{0:T(1024)S(1)} %bitcast.193), channel_id=1, replica_groups=mesh['row'=16,'col'=32] {'row'}, use_global_device_ids=true, to_apply=%region_35.36 | all-reduce | flops 2048 | bytes 16384 | tf_op jit(solution)/shard_map/psum | solution.py:126
  615.4 13.1 %while.106 = (s32[]{:T(128)}, f32[512]{0:T(512)S(1)}, s32[4]{0:T(128)S(1)}, f32[2048]{0:T(1024)S(1)}, f32[512]{0:T(512)S(1)}, /*index=5*/f32[2048]{0:T(1024)S(1)...) while((s32[]{:T(128)}, f32[512]{0:T(512)S(1)}, ...), condition=%wide.region_38.39_spmd.clone, body=%wide.region_36.38_spmd.clone.sunk | while | flops 136315392 | bytes 1596617 | solution.py:103
  628.5 57.4 %pmax.55 = f32[512]{0:T(512)S(1)} all-reduce(f32[512]{0:T(512)S(1)} %get-tuple-element.474), channel_id=1, replica_groups=mesh['row'=16,'col'=32] {'col'}, use_global_device_ids=true, to_apply=%region_39.40 | all-reduce | flops 512 | bytes 4096 | tf_op jit(solution)/shard_map/pmax | solution.py:106
  686.0 13.4 %while.107 = (s32[]{:T(128)}, f32[512]{0:T(512)S(1)}, s32[4]{0:T(128)S(1)}, f32[2048]{0:T(1024)S(1)}, f32[512]{0:T(512)S(1)}, /*index=5*/f32[2048]{0:T(1024)S(1)...) while((s32[]{:T(128)}, f32[512]{0:T(512)S(1)}, ...), condition=%wide.region_42.43_spmd.clone, body=%wide.region_40.42_spmd.clone.sunk | while | flops 136577536 | bytes 1598673 | solution.py:124
  703.7 4.4 collective-permute-start.16
  710.1 3.4 collective-permute-start.17
  715.5 4.3 collective-permute-start.18
  719.8 3.9 collective-permute-start.14
  723.7 5.2 collective-permute-start.19
  729.0 3.0 collective-permute-done.19
  732.6 41.6 %psum.31 = f32[]{:T(128)} all-reduce(f32[]{:T(128)} %get-tuple-element.1208), channel_id=1, replica_groups=mesh['row'=16,'col'=32] {'row'}, use_global_device_ids=true, to_apply=%region_44.45 | all-reduce | flops 1 | bytes 8 | tf_op jit(solution)/shard_map/psum | solution.py:135
  (264 shorter events, 104.6 us)
Async XLA Ops:
  6.5 89.2 %all-gather.3.cloned.1.call-start = ((), (), s32[]{:S(2)}) async-start(), calls=%async_computation | async-start | bytes 1114112 | tf_op jit(solution)/shard_map/all_gather | solution.py:64
  219.3 4.3 collective-permute-start
  223.7 5.8 collective-permute-start.1
  229.5 4.3 collective-permute-start.2
  233.8 43.6 %collective-permute-start.3 = (f32[512]{0:T(512)S(1)}, f32[512]{0:T(512)S(1)}, u32[]{:S(2)}, u32[]{:S(2)}) collective-permute-start(f32[512]{0:T(512)S(1)} %add.319), channel_id=1, source_target_pairs={{0,8},{1,9},{2,10},{3,11},{4,12},{5,13},{6,14},{7,15},{8,0},{9,1},... | collective-permute-start | bytes 6152 | tf_op jit(solution)/shard_map/ppermute | solution.py:15
  277.4 8.2 %collective-permute-start.4 = (f32[512]{0:T(512)S(1)}, f32[512]{0:T(512)S(1)}, u32[]{:S(2)}, u32[]{:S(2)}) collective-permute-start(f32[512]{0:T(512)S(1)} %add.320), channel_id=1, source_target_pairs={{0,16},{1,17},{2,18},{3,19},{4,20},{5,21},{6,22},{7,23},{8,24},{9,... | collective-permute-start | bytes 6152 | tf_op jit(solution)/shard_map/ppermute | solution.py:15
  397.2 4.3 collective-permute-start.5
  401.5 5.8 collective-permute-start.6
  407.3 4.3 collective-permute-start.7
  411.7 43.6 %collective-permute-start.8 = (f32[512]{0:T(512)S(1)}, f32[512]{0:T(512)S(1)}, u32[]{:S(2)}, u32[]{:S(2)}) collective-permute-start(f32[512]{0:T(512)S(1)} %add.326), channel_id=1, source_target_pairs={{0,8},{1,9},{2,10},{3,11},{4,12},{5,13},{6,14},{7,15},{8,0},{9,1},... | collective-permute-start | bytes 6152 | tf_op jit(solution)/shard_map/ppermute | solution.py:15
  455.3 8.2 %collective-permute-start.9 = (f32[512]{0:T(512)S(1)}, f32[512]{0:T(512)S(1)}, u32[]{:S(2)}, u32[]{:S(2)}) collective-permute-start(f32[512]{0:T(512)S(1)} %add.327), channel_id=1, source_target_pairs={{0,16},{1,17},{2,18},{3,19},{4,20},{5,21},{6,22},{7,23},{8,24},{9,... | collective-permute-start | bytes 6152 | tf_op jit(solution)/shard_map/ppermute | solution.py:15
  575.2 126.1 %collective-permute-start.10 = (f32[512]{0:T(512)S(1)}, f32[512]{0:T(512)S(1)}, u32[]{:S(2)}, u32[]{:S(2)}) collective-permute-start(f32[512]{0:T(512)S(1)} %get-tuple-element.472), channel_id=1, source_target_pairs={{0,1},{1,0},{2,3},{3,2},{4,5},{5,4},{6,7},{7,6},{8,9},{9,8},{10,11... | collective-permute-start | bytes 6152 | tf_op jit(solution)/shard_map/ppermute | solution.py:15
  699.4 4.3 collective-permute-start.15
  701.3 6.8 collective-permute-start.11
  703.7 6.4 collective-permute-start.16
  708.2 5.3 collective-permute-start.12
  710.1 5.3 collective-permute-start.17
  713.5 6.2 collective-permute-start.13
  715.5 8.2 %collective-permute-start.18 = (f32[512]{0:T(512)S(1)}, f32[512]{0:T(512)S(1)}, u32[]{:S(2)}, u32[]{:S(2)}) collective-permute-start(f32[512]{0:T(512)S(1)} %add.344), channel_id=1, source_target_pairs={{0,8},{1,9},{2,10},{3,11},{4,12},{5,13},{6,14},{7,15},{8,0},{9,1},... | collective-permute-start | bytes 6152 | tf_op jit(solution)/shard_map/ppermute | solution.py:15
  719.8 9.2 %collective-permute-start.14 = (f32[512]{0:T(512)S(1)}, f32[512]{0:T(512)S(1)}, u32[]{:S(2)}, u32[]{:S(2)}) collective-permute-start(f32[512]{0:T(512)S(1)} %add.336), channel_id=1, source_target_pairs={{0,16},{1,17},{2,18},{3,19},{4,20},{5,21},{6,22},{7,23},{8,24},{9,... | collective-permute-start | bytes 6152 | tf_op jit(solution)/shard_map/ppermute | solution.py:15
  723.7 8.2 %collective-permute-start.19 = (f32[512]{0:T(512)S(1)}, f32[512]{0:T(512)S(1)}, u32[]{:S(2)}, u32[]{:S(2)}) collective-permute-start(f32[512]{0:T(512)S(1)} %add.345), channel_id=1, source_target_pairs={{0,16},{1,17},{2,18},{3,19},{4,20},{5,21},{6,22},{7,23},{8,24},{9,... | collective-permute-start | bytes 6152 | tf_op jit(solution)/shard_map/ppermute | solution.py:15
Sparse Core Ops, SparseCore 0:
  9.5 47.9 all-gather.2
